TPU v7x, 32 devices: a whole 2x2x4 slice. The times are simulated.
32 devices in a mesh: tm: 8 (over y, x, core), row: 4 (over z).
Axes of the slice: x: 2, y: 2, z: 4, core: 2. Of those that a mesh axis runs over, the one named last changes fastest.
Arguments:
- pred_cov: bfloat16 [8, 1536, 1536], P('tm', 'row'), may hold values from -0.8 to 3.3, as said below
- cross: float32 [8, 1536, 1536], P('tm', 'row'), may hold values from -0.9 to 3.2
- filt_mean: float32 [8, 1536], P('tm', 'row'), may hold values from -6 to 6
- pred_mean: float32 [8, 1536], P('tm', 'row'), may hold values from -6 to 6
- next_smoothed: float32 [1536], P('row'), may hold values from -6 to 6
Outputs:
- smoothed: float32 [8, 1536], P('tm', 'row')
- gains: float32 [8, 1536, 1536], P('tm', 'row')
Inputs may be any that keep to these rules, and one draw needn't show every extreme that they name: `pred_cov`: each of the 8 matrices of size 1536 x 1536 is symmetric positive definite.
All inputs are finite; a program needn't handle non-finite values.
Results may differ from a plain program's by a relative error of at most 0.0003.
Values may be sent and summed in bfloat16 or wider, within the bound.
A program may use at most 128 MiB of HBM per device.

v0:
```python
import jax
import jax.numpy as jnp
from jax import lax
from jax.sharding import PartitionSpec as P

finest = lax.Precision.HIGHEST


def from_behind(array, axis, by):
    peers = lax.axis_size(axis)
    pairs = [(i, i + by) for i in range(peers) if 0 <= i + by < peers]
    return lax.ppermute(array, axis, pairs)


def matvec(matrix, vector):
    return jnp.dot(matrix, vector, precision=finest, preferred_element_type=jnp.float32)


def per_device(pred_cov, cross, filt_mean, pred_mean, next_smoothed):
    whole_cov = lax.all_gather(pred_cov, "row", axis=1, tiled=True)
    cholesky_factor = jnp.linalg.cholesky(whole_cov[0].astype(jnp.float32))
    gain = jax.scipy.linalg.cho_solve((cholesky_factor, True), cross[0].T).T
    steps = lax.axis_size("tm")
    final = lax.axis_index("tm") == steps - 1
    mean_f = filt_mean[0]
    mean_p = pred_mean[0]

    def advance(turn, state):
        later = from_behind(state, "tm", -1)
        later = jnp.where(final, next_smoothed, later)
        dispersion = lax.all_gather(later - mean_p, "row", axis=0, tiled=True)
        return mean_f + matvec(gain, dispersion)

    smoothed = lax.fori_loop(0, steps, advance, jnp.zeros_like(mean_f))
    return (smoothed[None, :], gain[None, :, :])


def solution(mesh):
    in_specs = (
        P("tm", "row", None),
        P("tm", "row", None),
        P("tm", "row"),
        P("tm", "row"),
        P("row"),
    )
    out_specs = (P("tm", "row"), P("tm", "row", None))
    return jax.shard_map(
        per_device, mesh=mesh, in_specs=in_specs, out_specs=out_specs, check_vma=False
    )
```

profile of v0, /device:TPU:0, one launch (start us, length us, event | category | flops | bytes accessed | tf_op | source)
XLA Modules:
  0.0 825.8 jit_solution(8059420826095659475)
XLA Ops:
  9.7 92.6 %all-gather.6.cloned.1.call-done = bf16[1,1536,1536]{1,2,0:T(8,128)(2,1)} async-done(((bf16[1,384,1536]{1,2,0:T(8,128)(2,1)}), bf16[1,1536,1536]{1,2,0:T(8,128)(2,1)}) %all-gather.6.cloned.1.call-update) | async-done | bytes 4718608 | tf_op jit(solution)/shard_map/all_gather | solution.py:20
  102.3 7.3 bitcast_convert_fusion
  109.6 9.6 %copy.12 = f32[1536,1536]{1,0:T(8,128)} copy(f32[1536,1536]{0,1:T(8,128)} %bitcast_convert_fusion) | data formatting | bytes 18874368 | tf_op jit(solution)/shard_map/convert_element_type | solution.py:21
  119.2 10.2 %fusion = f32[1536,1536]{1,0:T(8,128)} fusion(f32[1536,1536]{1,0:T(8,128)} %copy.12, bf16[1,1536,1536]{1,2,0:T(8,128)(2,1)} %all-gather.6.cloned.1.call-done), kind=kLoop, calls=%fused_computation.7 | loop fusion | flops 7077888 | bytes 23592960 | tf_op jit(solution)/shard_map/jit(cholesky)/div | solution.py:21
  130.2 11.7 %cholesky.341 = f32[128,128]{1,0:T(8,128)S(1)} custom-call(f32[128,128]{1,0:T(8,128)S(1)} %cholesky.892), custom_call_target="Cholesky" | custom-call | tf_op jit(solution)/shard_map/jit(cholesky)/cholesky | solution.py:21
  141.9 9.8 %custom-call.98 = f32[1,128,128]{1,2,0:T(8,128)S(1)} custom-call(f32[1,128,128]{2,1,0:T(8,128)S(1)} %get-tuple-element.202), custom_call_target="InvertDiagBlocksLowerTriangular" | custom-call | tf_op jit(solution)/shard_map/jit(cholesky)/cholesky | solution.py:21
  151.8 4.9 cholesky.371
  161.3 12.0 %cholesky.362 = f32[128,128]{1,0:T(8,128)S(1)} custom-call(f32[128,128]{1,0:T(8,128)S(1)} %cholesky.896), custom_call_target="Cholesky" | custom-call | tf_op jit(solution)/shard_map/jit(cholesky)/cholesky | solution.py:21
  174.0 9.8 %custom-call.99 = f32[1,128,128]{1,2,0:T(8,128)S(1)} custom-call(f32[1,128,128]{2,1,0:T(8,128)S(1)} %get-tuple-element.199), custom_call_target="InvertDiagBlocksLowerTriangular" | custom-call | tf_op jit(solution)/shard_map/jit(cholesky)/cholesky | solution.py:21
  188.2 11.7 %cholesky.385 = f32[128,128]{1,0:T(8,128)S(1)} custom-call(f32[128,128]{1,0:T(8,128)S(1)} %cholesky.901), custom_call_target="Cholesky" | custom-call | tf_op jit(solution)/shard_map/jit(cholesky)/cholesky | solution.py:21
  201.3 9.8 %custom-call.100 = f32[1,128,128]{1,2,0:T(8,128)S(1)} custom-call(f32[1,128,128]{2,1,0:T(8,128)S(1)} %get-tuple-element.196), custom_call_target="InvertDiagBlocksLowerTriangular" | custom-call | tf_op jit(solution)/shard_map/jit(cholesky)/cholesky | solution.py:21
  212.8 3.3 convolution_subtract_fusion
  216.1 11.7 %cholesky.715 = f32[128,128]{1,0:T(8,128)S(1)} custom-call(f32[128,128]{1,0:T(8,128)S(1)} %cholesky.906), custom_call_target="Cholesky" | custom-call | tf_op jit(solution)/shard_map/jit(cholesky)/cholesky | solution.py:21
  229.1 9.8 %custom-call.101 = f32[1,128,128]{1,2,0:T(8,128)S(1)} custom-call(f32[1,128,128]{2,1,0:T(8,128)S(1)} %get-tuple-element.193), custom_call_target="InvertDiagBlocksLowerTriangular" | custom-call | tf_op jit(solution)/shard_map/jit(cholesky)/cholesky | solution.py:21
  240.5 3.6 fusion.17
  244.0 11.9 %cholesky.734 = f32[128,128]{1,0:T(8,128)S(1)} custom-call(f32[128,128]{1,0:T(8,128)S(1)} %cholesky.911), custom_call_target="Cholesky" | custom-call | tf_op jit(solution)/shard_map/jit(cholesky)/cholesky | solution.py:21
  257.2 9.8 %custom-call.102 = f32[1,128,128]{1,2,0:T(8,128)S(1)} custom-call(f32[1,128,128]{2,1,0:T(8,128)S(1)} %get-tuple-element.190), custom_call_target="InvertDiagBlocksLowerTriangular" | custom-call | tf_op jit(solution)/shard_map/jit(cholesky)/cholesky | solution.py:21
  268.4 3.9 fusion.20
  272.3 11.7 %cholesky.754 = f32[128,128]{1,0:T(8,128)S(1)} custom-call(f32[128,128]{1,0:T(8,128)S(1)} %cholesky.916), custom_call_target="Cholesky" | custom-call | tf_op jit(solution)/shard_map/jit(cholesky)/cholesky | solution.py:21
  285.3 10.2 %custom-call.103 = f32[1,128,128]{1,2,0:T(8,128)S(1)} custom-call(f32[1,128,128]{2,1,0:T(8,128)S(1)} %get-tuple-element.187), custom_call_target="InvertDiagBlocksLowerTriangular" | custom-call | tf_op jit(solution)/shard_map/jit(cholesky)/cholesky | solution.py:21
  296.8 3.8 fusion.23
  300.6 11.7 %cholesky.774 = f32[128,128]{1,0:T(8,128)S(1)} custom-call(f32[128,128]{1,0:T(8,128)S(1)} %cholesky.921), custom_call_target="Cholesky" | custom-call | tf_op jit(solution)/shard_map/jit(cholesky)/cholesky | solution.py:21
  313.6 9.8 %custom-call.104 = f32[1,128,128]{1,2,0:T(8,128)S(1)} custom-call(f32[1,128,128]{2,1,0:T(8,128)S(1)} %get-tuple-element.184), custom_call_target="InvertDiagBlocksLowerTriangular" | custom-call | tf_op jit(solution)/shard_map/jit(cholesky)/cholesky | solution.py:21
  324.6 3.8 fusion.26
  328.4 11.9 %cholesky.794 = f32[128,128]{1,0:T(8,128)S(1)} custom-call(f32[128,128]{1,0:T(8,128)S(1)} %cholesky.926), custom_call_target="Cholesky" | custom-call | tf_op jit(solution)/shard_map/jit(cholesky)/cholesky | solution.py:21
  341.6 9.8 %custom-call.105 = f32[1,128,128]{1,2,0:T(8,128)S(1)} custom-call(f32[1,128,128]{2,1,0:T(8,128)S(1)} %get-tuple-element.181), custom_call_target="InvertDiagBlocksLowerTriangular" | custom-call | tf_op jit(solution)/shard_map/jit(cholesky)/cholesky | solution.py:21
  352.5 3.6 fusion.29
  356.1 11.7 %cholesky.814 = f32[128,128]{1,0:T(8,128)S(1)} custom-call(f32[128,128]{1,0:T(8,128)S(1)} %cholesky.931), custom_call_target="Cholesky" | custom-call | tf_op jit(solution)/shard_map/jit(cholesky)/cholesky | solution.py:21
  369.1 10.2 %custom-call.106 = f32[1,128,128]{1,2,0:T(8,128)S(1)} custom-call(f32[1,128,128]{2,1,0:T(8,128)S(1)} %get-tuple-element.178), custom_call_target="InvertDiagBlocksLowerTriangular" | custom-call | tf_op jit(solution)/shard_map/jit(cholesky)/cholesky | solution.py:21
  380.3 3.3 fusion.32
  383.6 11.7 %cholesky.834 = f32[128,128]{1,0:T(8,128)S(1)} custom-call(f32[128,128]{1,0:T(8,128)S(1)} %cholesky.936), custom_call_target="Cholesky" | custom-call | tf_op jit(solution)/shard_map/jit(cholesky)/cholesky | solution.py:21
  396.7 9.8 %custom-call.107 = f32[1,128,128]{1,2,0:T(8,128)S(1)} custom-call(f32[1,128,128]{2,1,0:T(8,128)S(1)} %get-tuple-element.175), custom_call_target="InvertDiagBlocksLowerTriangular" | custom-call | tf_op jit(solution)/shard_map/jit(cholesky)/cholesky | solution.py:21
  410.2 11.9 %cholesky.854 = f32[128,128]{1,0:T(8,128)S(1)} custom-call(f32[128,128]{1,0:T(8,128)S(1)} %cholesky.941), custom_call_target="Cholesky" | custom-call | tf_op jit(solution)/shard_map/jit(cholesky)/cholesky | solution.py:21
  423.4 9.8 %custom-call.108 = f32[1,128,128]{1,2,0:T(8,128)S(1)} custom-call(f32[1,128,128]{2,1,0:T(8,128)S(1)} %get-tuple-element.172), custom_call_target="InvertDiagBlocksLowerTriangular" | custom-call | tf_op jit(solution)/shard_map/jit(cholesky)/cholesky | solution.py:21
  436.2 11.7 %cholesky.872 = f32[128,128]{1,0:T(8,128)S(1)} custom-call(f32[128,128]{1,0:T(8,128)S(1)} %convolution_subtract_fusion.25), custom_call_target="Cholesky" | custom-call | tf_op jit(solution)/shard_map/jit(cholesky)/cholesky | solution.py:21
  457.5 8.6 %select_select_fusion = f32[1536,1536]{1,0:T(8,128)} fusion(f32[1536,1536]{1,0:T(8,128)} %get-tuple-element.170, pred[]{:T(512)S(6)} %cholesky.891), kind=kLoop, calls=%fused_computation.5 | loop fusion | flops 9437184 | bytes 18874368 | tf_op jit(solution)/shard_map/jit(_cho_solve)/triangular_solve | solution.py:22
  466.1 42.3 %while.12 = (s32[]{:T(128)}, f32[1536,1536]{1,0:T(8,128)}, s32[12,2]{0,1:T(2,128)S(1)}, f32[12,128,128]{2,1,0:T(8,128)}, s32[]{:T(128)}) while((s32[]{:T(128)}, f32[1536,1536]{1,0:T(8,128)}, s32[12,2]{0,1:T(2,128)S(1)}, f32[12,128,128]{2,1,0:T(8,128)}, s32[]{:T(128)}) %tuple.131), condition=%wide.while_cond, body=%wide.while_body.sunk | while | flops 2 | bytes 132705 | solution.py:22
  508.5 119.1 %custom-call.109 = f32[12,128,128]{1,2,0:T(8,128)S(1)} custom-call(f32[12,128,128]{2,1,0:T(8,128)} %get-tuple-element.47), custom_call_target="InvertDiagBlocksLowerTriangular" | custom-call | tf_op jit(solution)/shard_map/jit(_cho_solve)/triangular_solve | solution.py:22
  654.6 3.8 convolution_subtract_fusion.11
  679.0 136.0 %while.13 = (s32[]{:T(128)}, f32[384]{0:T(512)S(1)}, pred[]{:T(512)}, f32[384]{0:T(512)S(1)}, f32[384]{0:T(512)S(1)}, /*index=5*/f32[384,1536]{1,0:T(8,128)S(1)}, f32[384]{0:T(512)S(1)}, s32[]{:T(128)}, s32[]{:T(128)}) while((s32[]{:T(128)}, f32[384]{0:T(512)S(1)}, pred[]{:T(512)}, f32[384]{0:T(512)S(1)}, f32[384]{0:T(512)S(1)}, ...), condition=%wide.region_25.26_spmd.clone, body=%wide.region_24.25_spmd.clone.sunk | while | flops 7079427 | bytes 2397840 | solution.py:34
  682.1 11.9 %all-gather.3 = f32[4,1,384]{2,1,0:T(1,128)S(1)} all-gather(f32[1,1,384]{2,1,0:T(1,128)S(1)} %reshape.192), channel_id=1, replica_groups=mesh['tm'=8,'row'=4] {'row'}, dimensions={0}, use_global_device_ids=true | all-gather | bytes 7680 | tf_op jit(solution)/shard_map/while/body/eval_jaxpr/all_gather | solution.py:31
  699.1 11.9 %all-gather.3 = f32[4,1,384]{2,1,0:T(1,128)S(1)} all-gather(f32[1,1,384]{2,1,0:T(1,128)S(1)} %reshape.192), channel_id=1, replica_groups=mesh['tm'=8,'row'=4] {'row'}, dimensions={0}, use_global_device_ids=true | all-gather | bytes 7680 | tf_op jit(solution)/shard_map/while/body/eval_jaxpr/all_gather | solution.py:31
  716.1 11.9 %all-gather.3 = f32[4,1,384]{2,1,0:T(1,128)S(1)} all-gather(f32[1,1,384]{2,1,0:T(1,128)S(1)} %reshape.192), channel_id=1, replica_groups=mesh['tm'=8,'row'=4] {'row'}, dimensions={0}, use_global_device_ids=true | all-gather | bytes 7680 | tf_op jit(solution)/shard_map/while/body/eval_jaxpr/all_gather | solution.py:31
  733.1 11.9 %all-gather.3 = f32[4,1,384]{2,1,0:T(1,128)S(1)} all-gather(f32[1,1,384]{2,1,0:T(1,128)S(1)} %reshape.192), channel_id=1, replica_groups=mesh['tm'=8,'row'=4] {'row'}, dimensions={0}, use_global_device_ids=true | all-gather | bytes 7680 | tf_op jit(solution)/shard_map/while/body/eval_jaxpr/all_gather | solution.py:31
  750.1 11.9 %all-gather.3 = f32[4,1,384]{2,1,0:T(1,128)S(1)} all-gather(f32[1,1,384]{2,1,0:T(1,128)S(1)} %reshape.192), channel_id=1, replica_groups=mesh['tm'=8,'row'=4] {'row'}, dimensions={0}, use_global_device_ids=true | all-gather | bytes 7680 | tf_op jit(solution)/shard_map/while/body/eval_jaxpr/all_gather | solution.py:31
  767.1 11.9 %all-gather.3 = f32[4,1,384]{2,1,0:T(1,128)S(1)} all-gather(f32[1,1,384]{2,1,0:T(1,128)S(1)} %reshape.192), channel_id=1, replica_groups=mesh['tm'=8,'row'=4] {'row'}, dimensions={0}, use_global_device_ids=true | all-gather | bytes 7680 | tf_op jit(solution)/shard_map/while/body/eval_jaxpr/all_gather | solution.py:31
  784.0 11.9 %all-gather.3 = f32[4,1,384]{2,1,0:T(1,128)S(1)} all-gather(f32[1,1,384]{2,1,0:T(1,128)S(1)} %reshape.192), channel_id=1, replica_groups=mesh['tm'=8,'row'=4] {'row'}, dimensions={0}, use_global_device_ids=true | all-gather | bytes 7680 | tf_op jit(solution)/shard_map/while/body/eval_jaxpr/all_gather | solution.py:31
  801.0 11.9 %all-gather.3 = f32[4,1,384]{2,1,0:T(1,128)S(1)} all-gather(f32[1,1,384]{2,1,0:T(1,128)S(1)} %reshape.192), channel_id=1, replica_groups=mesh['tm'=8,'row'=4] {'row'}, dimensions={0}, use_global_device_ids=true | all-gather | bytes 7680 | tf_op jit(solution)/shard_map/while/body/eval_jaxpr/all_gather | solution.py:31
  (270 shorter events, 176.3 us)
Async XLA Ops:
  7.2 2.5 copy-start.4
  7.2 2.5 copy-start.5
  7.2 95.1 %all-gather.6.cloned.1.call-start = ((), (), s32[]{:S(2)}) async-start(), calls=%async_computation | async-start | bytes 5898240 | tf_op jit(solution)/shard_map/all_gather | solution.py:20
  457.5 170.1 %copy-start.2 = (f32[1,384,1536]{2,1,0:T(8,128)S(1)}, f32[1,384,1536]{2,1,0:T(8,128)}, u32[]{:S(2)}) copy-start(f32[1,384,1536]{2,1,0:T(8,128)} %param.8) | copy-start | bytes 7077892
  627.6 7.5 copy-start
  675.5 1.4 copy-start.1
  676.9 2.1 copy-start.3
  679.0 3.1 collective-permute-start
  696.0 3.1 collective-permute-start
  713.0 3.1 collective-permute-start
  730.0 3.1 collective-permute-start
  747.0 3.1 collective-permute-start
  764.0 3.1 collective-permute-start
  781.0 3.1 collective-permute-start
  798.0 3.1 collective-permute-start
Sparse Core Ops, SparseCore 0:
  10.2 92.0 all-gather.5
where the time goes:
time: 838 us; the launch traced here: 826 us
  other arithmetic  410 us (49%)
  matrix products  112 us (13%)
  waiting for transfers between devices  107 us (13%)
  blocking collectives  94.8 us (11%)
  local copies, waits for them, and re-layouts  68.2 us (8%)
  between operations  23.2 us (3%)
  starting transfers between devices  10.4 us (1%)
    another operation x46, other arithmetic, per_device(): cholesky_factor = jnp.linalg.cholesky(whole_cov[0].astype(jnp.float32))  265 us
    another operation x3, other arithmetic, per_device(): gain = jax.scipy.linalg.cho_solve((cholesky_factor, True), cross[0].T).T  128 us
    all_gather x8, blocking collectives, advance(): dispersion = lax.all_gather(later - mean_p, 'row', axis=0, tiled=True)  94.8 us
    all_gather x1, waiting for transfers between devices, per_device(): whole_cov = lax.all_gather(pred_cov, 'row', axis=1, tiled=True)  92.6 us
    another operation x22, matrix products, per_device(): cholesky_factor = jnp.linalg.cholesky(whole_cov[0].astype(jnp.float32))  50 us
    another operation x46, matrix products, per_device(): gain = jax.scipy.linalg.cho_solve((cholesky_factor, True), cross[0].T).T  46.2 us
    another operation x36, local copies, waits for them, and re-layouts  42.3 us
  transfers between devices with their start and end apart: 9, of which 9 were waited for; matrix products, arithmetic and copies ran while one was open for 0% of the time, Pallas kernels for 0%

commit v1 on v0

v1 whole, which is shorter than its diff:
```python
import functools

import jax
import jax.numpy as jnp
from jax import lax
from jax.experimental import pallas as pl
from jax.experimental.pallas import tpu as pltpu
from jax.sharding import PartitionSpec as P

finest = lax.Precision.HIGHEST
LANES = 128
CHUNK = 16
MOST_TURNS = 48
TOLERANCE = 2.0**-21


def from_behind(array, axis, by):
    peers = lax.axis_size(axis)
    pairs = [(i, i + by) for i in range(peers) if 0 <= i + by < peers]
    return lax.ppermute(array, axis, pairs)


def matvec(matrix, vector):
    return jnp.dot(matrix, vector, precision=finest, preferred_element_type=jnp.float32)


def folded(values):
    return sum(values[:, i : i + LANES] for i in range(0, values.shape[1], LANES))


def ratio(top, bottom):
    fine = bottom > 0.0
    return jnp.where(fine, top / jnp.where(fine, bottom, 1.0), 0.0)


def refine_kernel(cov, cross, gain, state, rest, image, way, partial, scale):
    rows, width = cross.shape
    tile = 256 if width % 256 == 0 else width
    chunks = rows // CHUNK
    unroll = 4 if chunks % 4 == 0 else 1

    def each_chunk(body):
        def step(i, carry):
            body(pl.ds(pl.multiple_of(i * CHUNK, CHUNK), CHUNK))
            return carry

        lax.fori_loop(0, chunks, step, 0, unroll=unroll)

    def begin(at):
        start = cross[at, :]
        rest[at, :] = start
        way[at, :] = start.astype(jnp.bfloat16)
        gain[at, :] = jnp.zeros_like(start)
        partial[at, :] = folded(start * start)

    each_chunk(begin)
    first = jnp.sum(partial[...], axis=1, keepdims=True)
    bound = first * (TOLERANCE * TOLERANCE)

    def excess(squares):
        return jnp.max(squares - bound)

    def advance(carry):
        turn, squares, _ = carry
        partial[...] = jnp.zeros_like(partial)

        def column(j, unused):
            at = pl.ds(pl.multiple_of(j * tile, tile), tile)
            product = jnp.dot(way[...], cov[:, at], preferred_element_type=jnp.float32)
            image[:, at] = product
            partial[...] += folded(product * way[:, at].astype(jnp.float32))
            return unused

        lax.fori_loop(0, width // tile, column, 0)
        length = ratio(squares, jnp.sum(partial[...], axis=1, keepdims=True))
        scale[...] = jnp.broadcast_to(length, scale.shape)

        def move(at):
            by = scale[at, :][:, :1]
            gain[at, :] += by * way[at, :].astype(jnp.float32)
            left = rest[at, :] - by * image[at, :]
            rest[at, :] = left
            partial[at, :] = folded(left * left)

        each_chunk(move)
        fresh = jnp.sum(partial[...], axis=1, keepdims=True)
        scale[...] = jnp.broadcast_to(ratio(fresh, squares), scale.shape)

        def turn_way(at):
            by = scale[at, :][:, :1]
            ahead = rest[at, :] + by * way[at, :].astype(jnp.float32)
            way[at, :] = ahead.astype(jnp.bfloat16)

        each_chunk(turn_way)
        return turn + 1, fresh, excess(fresh)

    def unfinished(carry):
        turn, _, over = carry
        return jnp.logical_and(turn < MOST_TURNS, jnp.logical_not(over <= 0.0))

    _, _, over = lax.while_loop(unfinished, advance, (jnp.int32(0), first, excess(first)))
    state[0, 0] = jnp.where(over <= 0.0, 1, 0)


def refine(cov, cross):
    rows, width = cross.shape
    vmem = pl.BlockSpec(memory_space=pltpu.VMEM)
    return pl.pallas_call(
        refine_kernel,
        out_shape=(
            jax.ShapeDtypeStruct((rows, width), jnp.float32),
            jax.ShapeDtypeStruct((1, 1), jnp.int32),
        ),
        in_specs=[vmem, vmem],
        out_specs=(vmem, pl.BlockSpec(memory_space=pltpu.SMEM)),
        scratch_shapes=[
            pltpu.VMEM((rows, width), jnp.float32),
            pltpu.VMEM((rows, width), jnp.float32),
            pltpu.VMEM((rows, width), jnp.bfloat16),
            pltpu.VMEM((rows, LANES), jnp.float32),
            pltpu.VMEM((rows, LANES), jnp.float32),
        ],
        compiler_params=pltpu.CompilerParams(vmem_limit_bytes=48 * 2**20),
        cost_estimate=pl.CostEstimate(
            flops=32 * rows * width * width, bytes_accessed=16 * rows * width, transcendentals=0
        ),
    )(cov, cross)


def direct(cov, cross):
    cholesky_factor = jnp.linalg.cholesky(cov.astype(jnp.float32))
    return jax.scipy.linalg.cho_solve((cholesky_factor, True), cross.T).T


def backward_kernel(steps, peers, gain, mean_f, mean_p, ahead, out, means, later, mean_sent, mean_came, sent, came):
    t = lax.axis_index("tm")
    me = lax.axis_index("row")
    width = mean_f.shape[1]
    final = t == steps - 1

    def other(k):
        return lax.rem(me + k, peers)

    def greet(step, row):
        pl.semaphore_signal(
            pltpu.get_barrier_semaphore(),
            inc=1,
            device_id=(step, row),
            device_id_type=pl.DeviceIdType.MESH,
        )

    for k in range(1, peers):
        greet(t, other(k))

    @pl.when(t > 0)
    def _():
        for k in range(peers):
            greet(t - 1, other(k))

    @pl.when(jnp.logical_not(final))
    def _():
        for k in range(peers):
            greet(t + 1, other(k))

    greeters = jnp.where(jnp.logical_or(t == 0, final), 2 * peers - 1, 3 * peers - 1)
    pl.semaphore_wait(pltpu.get_barrier_semaphore(), greeters)

    def copy(source, target, slot, sends, comes, k, step, row):
        return pltpu.make_async_remote_copy(
            src_ref=source,
            dst_ref=target.at[slot],
            send_sem=sends.at[k],
            recv_sem=comes.at[slot],
            device_id=(step, row),
            device_id_type=pl.DeviceIdType.MESH,
        )

    for k in range(1, peers):
        copy(mean_p, means, me, mean_sent, mean_came, k, t, other(k)).start()
    means[pl.ds(me, 1)] = mean_p[...][None]

    @pl.when(final)
    def _():
        for k in range(1, peers):
            copy(ahead, later, me, sent, came, k, t, other(k)).start()
        later[pl.ds(me, 1)] = ahead[...][None]
        for k in range(1, peers):
            copy(ahead, later, me, sent, came, k, t, other(k)).wait_send()

    for k in range(1, peers):
        copy(mean_p, means, me, mean_sent, mean_came, k, t, other(k)).wait_send()
    for k in range(1, peers):
        copy(mean_p, means, other(k), mean_sent, mean_came, k, t, other(k)).wait_recv()

    @pl.when(jnp.logical_not(final))
    def _():
        copy(ahead, later, me, sent, came, 0, t + 1, me).wait_recv()

    for k in range(1, peers):
        copy(ahead, later, other(k), sent, came, k, t, other(k)).wait_recv()

    total = jnp.zeros((width, LANES), jnp.float32)
    for j in range(peers):
        innovation = later[j] - means[j]
        for i in range(0, width, LANES):
            total += gain[:, j * width + i : j * width + i + LANES] * innovation[:, i : i + LANES]
    out[...] = mean_f[...] + jnp.sum(total.T, axis=0, keepdims=True)

    @pl.when(t > 0)
    def _():
        for k in range(peers):
            copy(out, later, me, sent, came, k, t - 1, other(k)).start()
        for k in range(peers):
            copy(out, later, me, sent, came, k, t - 1, other(k)).wait_send()


def backward(gain, mean_f, mean_p, ahead):
    steps, peers = lax.axis_size("tm"), lax.axis_size("row")
    width = mean_f.shape[1]
    vmem = pl.BlockSpec(memory_space=pltpu.VMEM)
    return pl.pallas_call(
        functools.partial(backward_kernel, steps, peers),
        out_shape=jax.ShapeDtypeStruct((1, width), jnp.float32),
        in_specs=[vmem] * 4,
        out_specs=vmem,
        scratch_shapes=[
            pltpu.VMEM((peers, 1, width), jnp.float32),
            pltpu.VMEM((peers, 1, width), jnp.float32),
            pltpu.SemaphoreType.DMA((peers,)),
            pltpu.SemaphoreType.DMA((peers,)),
            pltpu.SemaphoreType.DMA((peers,)),
            pltpu.SemaphoreType.DMA((peers,)),
        ],
        compiler_params=pltpu.CompilerParams(
            collective_id=1, has_side_effects=True, vmem_limit_bytes=32 * 2**20
        ),
        cost_estimate=pl.CostEstimate(
            flops=2 * width * width * peers, bytes_accessed=4 * width * width * peers, transcendentals=0
        ),
    )(gain, mean_f, mean_p, ahead)


def backward_by_collectives(gain, mean_f, mean_p, ahead):
    steps = lax.axis_size("tm")
    final = lax.axis_index("tm") == steps - 1

    def advance(turn, state):
        later = from_behind(state, "tm", -1)
        later = jnp.where(final, ahead[0], later)
        dispersion = lax.all_gather(later - mean_p[0], "row", axis=0, tiled=True)
        return mean_f[0] + matvec(gain, dispersion)

    return lax.fori_loop(0, steps, advance, jnp.zeros_like(mean_f[0]))[None, :]


def per_device(pred_cov, cross, filt_mean, pred_mean, next_smoothed):
    whole_cov = lax.all_gather(pred_cov, "row", axis=1, tiled=True)[0]
    found, state = refine(whole_cov, cross[0])
    gain = lax.cond(
        state[0, 0] == 1, lambda cov, part, found: found, lambda cov, part, found: direct(cov, part),
        whole_cov, cross[0], found,
    )
    aligned = filt_mean.shape[1] % LANES == 0
    sweep = backward if aligned else backward_by_collectives
    smoothed = sweep(gain, filt_mean, pred_mean, next_smoothed[None, :])
    return (smoothed, gain[None, :, :])


def solution(mesh):
    in_specs = (
        P("tm", "row", None),
        P("tm", "row", None),
        P("tm", "row"),
        P("tm", "row"),
        P("row"),
    )
    out_specs = (P("tm", "row"), P("tm", "row", None))
    return jax.shard_map(
        per_device, mesh=mesh, in_specs=in_specs, out_specs=out_specs, check_vma=False
    )
```

time: 838 us -> 226 us (0.27); the launches traced: 826 us -> 226 us
  other arithmetic: 410 us -> 0 us
  Pallas kernels: 0 us -> 115 us
  matrix products: 112 us -> 0 us
  blocking collectives: 94.8 us -> 0 us
  local copies, waits for them, and re-layouts: 68.2 us -> 1.7 us
  waiting for transfers between devices: 107 us -> 93.8 us
  starting transfers between devices: 10.4 us -> 0.04 us
  between operations: 23.2 us -> 14.7 us
    another operation x49 -> x0, other arithmetic: 392 us -> none  [the longest x46 265 us: per_device(): cholesky_factor = jnp.linalg.cholesky(whole_cov[0].astype(jnp.float32))]
    pallas_call x0 -> x2, Pallas kernels: none -> 115 us  [the longest x1 84.2 us: refine(): pl.pallas_call(refine_kernel, out_shape=(jax.ShapeDtypeStruct((rows, widt...]
    another operation x68 -> x0, matrix products: 96.2 us -> none  [the longest x22 50 us: per_device(): cholesky_factor = jnp.linalg.cholesky(whole_cov[0].astype(jnp.float32))]
    all_gather x8 -> x0, blocking collectives: 94.8 us -> none  [advance(): dispersion = lax.all_gather(later - mean_p, 'row', axis=0, tiled=True)]
    another operation x57 -> x0, local copies, waits for them, and re-layouts: 48.3 us -> none
    dot_general x8 -> x0, matrix products: 16.3 us -> none  [matvec(): jnp.dot(matrix, vector, precision=finest, preferred_element_type=jnp.floa...]
    ppermute x8 -> x0, waiting for transfers between devices: 14 us -> none  [from_behind(): return lax.ppermute(array, axis, pairs)]
    ppermute x8 -> x0, starting transfers between devices: 10.3 us -> none  [from_behind(): return lax.ppermute(array, axis, pairs)]
  transfers between devices with their start and end apart: 9 -> 1, of which waited for: 9 -> 1; matrix products, arithmetic and copies ran while one was open for 0% -> 0% of each run, Pallas kernels for 0% -> 0%
where the time goes in v1:
time: 226 us
  Pallas kernels  115 us (51%)
  waiting for transfers between devices  93.8 us (42%)
  between operations  14.7 us (7%)
    all_gather x1, waiting for transfers between devices, per_device(): whole_cov = lax.all_gather(pred_cov, 'row', axis=1, tiled=True)[0]  93.1 us
    pallas_call x1, Pallas kernels, refine(): pl.pallas_call(refine_kernel, out_shape=(jax.ShapeDtypeStruct((rows, widt...  84.2 us
    pallas_call x1, Pallas kernels, backward(): pl.pallas_call(functools.partial(backward_kernel, steps, peers), out_shap...  31.2 us
  transfers between devices with their start and end apart: 1, of which 1 were waited for; matrix products, arithmetic and copies ran while one was open for 0% of the time, Pallas kernels for 0%

profile of v1, /device:TPU:0, one launch (start us, length us, event | category | flops | bytes accessed | tf_op | source)
XLA Modules:
  0.0 225.9 jit_solution(17717432032258896049)
XLA Ops:
  7.2 0.0 all-gather.2.cloned.1.call-start
  7.2 0.7 all-gather.2.cloned.1.call-update
  7.9 0.7 broadcast_in_dim.8.ahead
  8.6 93.1 %all-gather.2.cloned.1.call-done = bf16[1,1536,1536]{2,1,0:T(8,128)(2,1)} async-done(((bf16[1,384,1536]{2,1,0:T(8,128)(2,1)}), bf16[1,1536,1536]{2,1,0:T(8,128)(2,1)}) %all-gather.2.cloned.1.call-update) | async-done | bytes 4718608 | tf_op jit(solution)/shard_map/all_gather | solution.py:257
  101.7 0.0 copy-start.3
  101.7 84.2 %shard_map.68 = (f32[384,1536]{1,0:T(8,128)}, s32[1,1]{1,0:T(1,128)}) custom-call(bf16[1536,1536]{1,0:T(8,128)(2,1)} %bitcast.201, f32[384,1536]{1,0:T(8,128)} %bitcast.205), custom_call_target="tpu_custom_call" | custom-call | flops 28991029248 | bytes 9437184 | tf_op jit(solution)/shard_map/pallas_call | solution.py:108
  186.6 0.0 copy-done.3
  186.6 0.0 copy-start
  186.6 0.0 copy-start.1
  186.6 0.2 conditional.1
  186.9 0.4 copy-done
  187.3 0.0 copy-done.1
  187.3 31.2 %shard_map.69 = f32[1,384]{1,0:T(1,128)S(1)} custom-call(f32[384,1536]{1,0:T(8,128)} %get-tuple-element.26.gain, f32[1,384]{1,0:T(1,128)S(1)} %copy-done, f32[1,384]{1,0:T(1,128)S(1)} %copy-done.1, f32[1,384]{1,0:T(1,128)S(1)} %broadcast_in_dim.8.ahead), custom_call_target="tpu_custom_call" | custom-call | flops 1179648 | bytes 2359296 | tf_op jit(solution)/shard_map/pallas_call | solution.py:221
  218.5 0.6 copy.157
Async XLA Ops:
  7.2 94.5 %all-gather.2.cloned.1.call-start = ((), (), s32[]{:S(2)}) async-start(), calls=%async_computation | async-start | bytes 5898240 | tf_op jit(solution)/shard_map/all_gather | solution.py:257
  101.7 84.9 %copy-start.3 = (f32[1,384,1536]{2,1,0:T(8,128)S(1)}, f32[1,384,1536]{2,1,0:T(8,128)}, u32[]{:S(2)}) copy-start(f32[1,384,1536]{2,1,0:T(8,128)} %param.8) | copy-start | bytes 7077892
  186.6 0.7 copy-start
  186.6 0.7 copy-start.1
Sparse Core Ops, SparseCore 0:
  9.6 92.0 all-gather.1
